TPU v7x, 32 devices: a whole 2x2x4 slice. The times are simulated.
32 devices in a mesh: chan: 8 (over z, x), freq: 4 (over y, core).
Axes of the slice: x: 2, y: 2, z: 4, core: 2. Of those that a mesh axis runs over, the one named last changes fastest.
Arguments:
- strain: bfloat16 [512, 256, 1024], P('chan', 'freq'), may hold values from -6 to 6
- mad_index: int32 [512], P('chan'), may hold values from 0 to 15
- mad_table: float32 [16], replicated, may hold values from 0.25 to 2.5
- freq_bins: int32 [64], replicated, may hold values from 1 to 511
- valid_count: int32 [512], P('chan'), may hold values from 64 to 256
Outputs:
- cross: float32 [64, 2, 512, 512], P('freq', None, 'chan')
All inputs are finite; a program needn't handle non-finite values.
Results may differ from a plain program's by a relative error of at most 0.0057.
Values may be sent and summed in bfloat16 or wider, within the bound.
A program may use at most 256 MiB of HBM per device.

v0:
```python
import math

import jax
import jax.numpy as jnp
from jax import lax
from jax.sharding import PartitionSpec as P

CLIP_FACTOR = 2.0


def passed_along(block, axis, distance):
    devices = range(lax.axis_size(axis))
    route = [((i - distance) % len(devices), i) for i in devices]
    return lax.ppermute(block, axis, route)


def dft_table(freq_bins, length):
    samples = jnp.arange(length, dtype=jnp.int32)
    phase_index = samples[:, None] * freq_bins[None, :] % length
    angle = phase_index.astype(jnp.float32) * (2.0 * math.pi / length)
    taper = 0.5 - 0.5 * jnp.cos(samples.astype(jnp.float32) * (2.0 * math.pi / length))
    cosine = taper[:, None] * jnp.cos(angle)
    sine = -taper[:, None] * jnp.sin(angle)
    stacked = jnp.stack([cosine, sine], axis=2)
    return stacked.reshape(length, 2 * freq_bins.shape[0]).astype(jnp.bfloat16)


def clip_scales(mad_index, mad_table):
    entries = jnp.arange(mad_table.shape[0], dtype=jnp.int32)
    matches = mad_index[:, None] == entries[None, :]
    return jnp.sum(jnp.where(matches, mad_table[None, :], 0.0), axis=1)


def cross_block(own_panel, visitor):
    bin_count, _, row_count, win_count = own_panel.shape
    col_count = visitor.shape[2]
    products = jnp.einsum(
        "fcw,fdw->fcd",
        own_panel.reshape(bin_count, 2 * row_count, win_count),
        visitor.reshape(bin_count, 2 * col_count, win_count),
        preferred_element_type=jnp.float32,
    )
    products = products.reshape(bin_count, 2, row_count, 2, col_count)
    real_part = products[:, 0, :, 0] + products[:, 1, :, 1]
    imag_part = products[:, 1, :, 0] - products[:, 0, :, 1]
    return jnp.stack([real_part, imag_part], axis=1)


def place_block(result, block, column_first):
    return lax.dynamic_update_slice(result, block, (0, 0, 0, column_first))


def per_device(strain, mad_index, mad_table, freq_bins, valid_count):
    channels, win_local, length = strain.shape
    bin_count = freq_bins.shape[0]
    limits = (clip_scales(mad_index, mad_table) * CLIP_FACTOR)[:, None, None]
    clipped = jnp.clip(strain.astype(jnp.float32), -limits, limits).astype(jnp.bfloat16)
    table = dft_table(freq_bins, length)
    flat_rows = clipped.reshape(channels * win_local, length)
    spectrum = lax.dot_general(
        table, flat_rows, (((0,), (1,)), ((), ())), preferred_element_type=jnp.float32
    )
    window_ids = lax.axis_index("freq") * win_local + jnp.arange(win_local, dtype=jnp.int32)
    counts = valid_count.astype(jnp.float32)
    weights = jnp.where(
        window_ids[None, :] < valid_count[:, None], 1.0 / jnp.sqrt(counts)[:, None], 0.0
    )
    weighted = (spectrum * weights.reshape(1, channels * win_local)).astype(jnp.bfloat16)
    weighted = weighted.reshape(bin_count, 2, channels, win_local)
    panels = lax.all_to_all(weighted, "freq", split_axis=0, concat_axis=3, tiled=True)
    cycle_size = lax.axis_size("chan")
    my_index = lax.axis_index("chan")
    bin_local = panels.shape[0]
    output = jnp.zeros((bin_local, 2, channels, cycle_size * channels), jnp.float32)
    output = place_block(output, cross_block(panels, panels), my_index * channels)

    def step_one(step_idx, carry):
        visitor, result = carry
        visitor = passed_along(visitor, "chan", 1)
        source = (my_index - step_idx) % cycle_size
        return (visitor, place_block(result, cross_block(panels, visitor), source * channels))

    _, output = lax.fori_loop(1, cycle_size, step_one, (panels, output))
    return output


def solution(mesh):
    return jax.shard_map(
        per_device,
        mesh=mesh,
        in_specs=(P("chan", "freq", None), P("chan"), P(), P(), P("chan")),
        out_specs=P("freq", None, "chan", None),
        check_vma=False,
    )
```

profile of v0, /device:TPU:0, one launch (start us, length us, event | category | flops | bytes accessed | tf_op | source)
XLA Modules:
  0.0 351.3 jit_solution(8300555231827465210)
XLA Ops:
  0.0 1.9 multiply_convert_fusion.1
  4.6 10.6 %minimum_convert_fusion = bf16[64,64,1024]{2,1,0:T(8,128)(2,1)} fusion(bf16[64,64,1024]{2,1,0:T(8,128)(2,1)} %param.7, bf16[64]{0:T(256)(128)(2,1)S(1)} %get-tuple-element.160, bf16[64]{0:T(256)(128)(2,1)S(1)} %get-tuple-element.159), kind=kLoop, calls=%fused_computation.3 | loop fusion | flops 25165824 | bytes 16777472 | tf_op jit(solution)/shard_map/convert_element_type | solution.py:57
  15.2 6.3 %fusion = bf16[128,4096]{1,0:T(8,128)(2,1)S(1)} fusion(bf16[1024,128]{0,1:T(8,128)(2,1)S(1)} %convert_element_type.50, bf16[4096,1024]{1,0:T(8,128)(2,1)} %bitcast.54, f32[4096]{0:T(1024)S(1)} %select_n.68), kind=kOutput, calls=%fused_computation.5 | convolution fusion | flops 1074790400 | bytes 9715712 | tf_op jit(solution)/shard_map/dot_general | solution.py:60
  21.5 2.3 reshape.338
  23.8 2.7 reshape.341
  26.5 4.2 %all-to-all-start = ((bf16[4,2,65536]{2,1,0:T(2,128)(2,1)}), bf16[4,2,65536]{2,1,0:T(2,128)(2,1)S(1)}, u32[]{:S(2)}, u32[]{:S(2)}) async-start(bf16[4,2,65536]{2,1,0:T(2,128)(2,1)} %reshape.341), calls=%async_computation | async-start | bytes 2097152 | tf_op jit(solution)/shard_map/all_to_all | solution.py:70
  30.7 14.5 %all-to-all-done = bf16[4,2,65536]{2,1,0:T(2,128)(2,1)S(1)} async-done(((bf16[4,2,65536]{2,1,0:T(2,128)(2,1)}), bf16[4,2,65536]{2,1,0:T(2,128)(2,1)S(1)}, u32[]{:S(2)}, u32[]{:S(2)}) %all-to-all-start) | async-done | bytes 1048608 | tf_op jit(solution)/shard_map/all_to_all | solution.py:70
  45.2 2.7 reshape.342
  47.9 3.6 %copy.56 = bf16[4,16,2,64,64]{4,0,3,2,1:T(4,128)(2,1)S(1)} copy(bf16[4,16,2,64,64]{4,3,2,1,0:T(8,128)(2,1)} %bitcast.57) | data formatting | bytes 2097152 | tf_op jit(solution)/shard_map/all_to_all | solution.py:70
  51.4 1.4 reshape.339
  52.8 2.2 all_to_all.16
  55.0 1.4 fusion.12
  56.4 2.5 reshape.340
  58.9 2.3 fusion.10
  61.2 1.2 copy.60
  62.6 2.5 broadcast_in_dim.42
  65.1 5.9 %dynamic_update_slice.13 = f32[16,2,64,512]{3,2,0,1:T(8,128)} dynamic-update-slice(f32[16,2,64,512]{3,2,0,1:T(8,128)} %broadcast_in_dim.42, f32[16,2,64,64]{3,2,0,1:T(8,128)S(1)} %pad_maximum_fusion.1, s32[]{:T(128)} %constant.92.clone.1, s32[]{:T(128)} %constant.92.clone.1, s32[]{:T(128)} %constant.92.clone.1, s32[]{:T(128)S(6)} %select_n.69) | dynamic-update-slice | bytes 1048580 | tf_op jit(solution)/shard_map/dynamic_update_slice | solution.py:50
  71.0 275.4 %while.17 = (s32[]{:T(128)}, bf16[16,2,64,256]{3,2,1,0:T(8,128)(2,1)S(1)}, f32[16,2,64,512]{3,2,0,1:T(8,128)}, bf16[16,2,64,256]{3,2,1,0:T(8,128)(2,1)}, s32[]{:...) while((s32[]{:T(128)}, ...), condition=%wide.region_2.3_spmd, body=%wide.region_1.2_spmd.sunk | while | flops 134479872 | bytes 25690480 | solution.py:83
  71.0 5.1 %collective-permute-start = (bf16[16,2,64,256]{3,2,1,0:T(8,128)(2,1)S(1)}, bf16[16,2,64,256]{3,2,1,0:T(8,128)(2,1)S(1)}, u32[]{:S(2)}, u32[]{:S(2)}) collective-permute-start(bf16[16,2,64,256]{3,2,1,0:T(8,128)(2,1)S(1)} %get-tuple-element.220), channel_id=1, source_target_pairs={{28,0},{0,4},{4,8},{8,12},{12,16},{16,20},{20,24},{24,28},{29,1},{... | collective-permute-start | bytes 3145736 | tf_op jit(solution)/shard_map/while/body/eval_jaxpr/ppermute | solution.py:14
  76.1 25.3 %collective-permute-done = bf16[16,2,64,256]{3,2,1,0:T(8,128)(2,1)S(1)} collective-permute-done((bf16[16,2,64,256]{3,2,1,0:T(8,128)(2,1)S(1)}, bf16[16,2,64,256]{3,2,1,0:T(8,128)(2,1)S(1)}, u32[]{:S(2)}, u32[]{:S(2)}) %collective-permute-start) | collective-permute-done | bytes 1048608 | tf_op jit(solution)/shard_map/while/body/eval_jaxpr/ppermute | solution.py:14
  102.3 1.7 fusion.25
  105.2 2.3 fusion.26
  107.8 8.1 %dynamic_update_slice.15 = f32[16,2,64,512]{3,2,0,1:T(8,128)} dynamic-update-slice(f32[16,2,64,512]{3,2,0,1:T(8,128)} %get-tuple-element.221, f32[16,2,64,64]{3,2,0,1:T(8,128)S(1)} %pad_maximum_fusion.4, s32[]{:T(128)} %constant.92.clone.1..sunk, s32[]{:T(128)} %constant.92.clone.1..sunk, s32[]{:T(128)} %constant.92.clone.1..sunk, s32[]{:T(128)S(6)} %select_n.84) | dynamic-update-slice | bytes 1048580 | tf_op jit(solution)/shard_map/while/body/eval_jaxpr/dynamic_update_slice | solution.py:50
  116.1 26.8 %collective-permute-done = bf16[16,2,64,256]{3,2,1,0:T(8,128)(2,1)S(1)} collective-permute-done((bf16[16,2,64,256]{3,2,1,0:T(8,128)(2,1)S(1)}, bf16[16,2,64,256]{3,2,1,0:T(8,128)(2,1)S(1)}, u32[]{:S(2)}, u32[]{:S(2)}) %collective-permute-start) | collective-permute-done | bytes 1048608 | tf_op jit(solution)/shard_map/while/body/eval_jaxpr/ppermute | solution.py:14
  143.8 1.7 fusion.25
  146.6 2.3 fusion.26
  149.3 5.3 %dynamic_update_slice.15 = f32[16,2,64,512]{3,2,0,1:T(8,128)} dynamic-update-slice(f32[16,2,64,512]{3,2,0,1:T(8,128)} %get-tuple-element.221, f32[16,2,64,64]{3,2,0,1:T(8,128)S(1)} %pad_maximum_fusion.4, s32[]{:T(128)} %constant.92.clone.1..sunk, s32[]{:T(128)} %constant.92.clone.1..sunk, s32[]{:T(128)} %constant.92.clone.1..sunk, s32[]{:T(128)S(6)} %select_n.84) | dynamic-update-slice | bytes 1048580 | tf_op jit(solution)/shard_map/while/body/eval_jaxpr/dynamic_update_slice | solution.py:50
  155.1 25.5 %collective-permute-done = bf16[16,2,64,256]{3,2,1,0:T(8,128)(2,1)S(1)} collective-permute-done((bf16[16,2,64,256]{3,2,1,0:T(8,128)(2,1)S(1)}, bf16[16,2,64,256]{3,2,1,0:T(8,128)(2,1)S(1)}, u32[]{:S(2)}, u32[]{:S(2)}) %collective-permute-start) | collective-permute-done | bytes 1048608 | tf_op jit(solution)/shard_map/while/body/eval_jaxpr/ppermute | solution.py:14
  181.6 1.7 fusion.25
  184.4 2.3 fusion.26
  187.1 8.9 %dynamic_update_slice.15 = f32[16,2,64,512]{3,2,0,1:T(8,128)} dynamic-update-slice(f32[16,2,64,512]{3,2,0,1:T(8,128)} %get-tuple-element.221, f32[16,2,64,64]{3,2,0,1:T(8,128)S(1)} %pad_maximum_fusion.4, s32[]{:T(128)} %constant.92.clone.1..sunk, s32[]{:T(128)} %constant.92.clone.1..sunk, s32[]{:T(128)} %constant.92.clone.1..sunk, s32[]{:T(128)S(6)} %select_n.84) | dynamic-update-slice | bytes 1048580 | tf_op jit(solution)/shard_map/while/body/eval_jaxpr/dynamic_update_slice | solution.py:50
  196.1 24.9 %collective-permute-done = bf16[16,2,64,256]{3,2,1,0:T(8,128)(2,1)S(1)} collective-permute-done((bf16[16,2,64,256]{3,2,1,0:T(8,128)(2,1)S(1)}, bf16[16,2,64,256]{3,2,1,0:T(8,128)(2,1)S(1)}, u32[]{:S(2)}, u32[]{:S(2)}) %collective-permute-start) | collective-permute-done | bytes 1048608 | tf_op jit(solution)/shard_map/while/body/eval_jaxpr/ppermute | solution.py:14
  222.0 1.7 fusion.25
  224.9 2.3 fusion.26
  227.5 6.0 %dynamic_update_slice.15 = f32[16,2,64,512]{3,2,0,1:T(8,128)} dynamic-update-slice(f32[16,2,64,512]{3,2,0,1:T(8,128)} %get-tuple-element.221, f32[16,2,64,64]{3,2,0,1:T(8,128)S(1)} %pad_maximum_fusion.4, s32[]{:T(128)} %constant.92.clone.1..sunk, s32[]{:T(128)} %constant.92.clone.1..sunk, s32[]{:T(128)} %constant.92.clone.1..sunk, s32[]{:T(128)S(6)} %select_n.84) | dynamic-update-slice | bytes 1048580 | tf_op jit(solution)/shard_map/while/body/eval_jaxpr/dynamic_update_slice | solution.py:50
  234.1 23.5 %collective-permute-done = bf16[16,2,64,256]{3,2,1,0:T(8,128)(2,1)S(1)} collective-permute-done((bf16[16,2,64,256]{3,2,1,0:T(8,128)(2,1)S(1)}, bf16[16,2,64,256]{3,2,1,0:T(8,128)(2,1)S(1)}, u32[]{:S(2)}, u32[]{:S(2)}) %collective-permute-start) | collective-permute-done | bytes 1048608 | tf_op jit(solution)/shard_map/while/body/eval_jaxpr/ppermute | solution.py:14
  258.6 1.7 fusion.25
  261.5 2.3 fusion.26
  264.1 8.8 %dynamic_update_slice.15 = f32[16,2,64,512]{3,2,0,1:T(8,128)} dynamic-update-slice(f32[16,2,64,512]{3,2,0,1:T(8,128)} %get-tuple-element.221, f32[16,2,64,64]{3,2,0,1:T(8,128)S(1)} %pad_maximum_fusion.4, s32[]{:T(128)} %constant.92.clone.1..sunk, s32[]{:T(128)} %constant.92.clone.1..sunk, s32[]{:T(128)} %constant.92.clone.1..sunk, s32[]{:T(128)S(6)} %select_n.84) | dynamic-update-slice | bytes 1048580 | tf_op jit(solution)/shard_map/while/body/eval_jaxpr/dynamic_update_slice | solution.py:50
  273.2 23.1 %collective-permute-done = bf16[16,2,64,256]{3,2,1,0:T(8,128)(2,1)S(1)} collective-permute-done((bf16[16,2,64,256]{3,2,1,0:T(8,128)(2,1)S(1)}, bf16[16,2,64,256]{3,2,1,0:T(8,128)(2,1)S(1)}, u32[]{:S(2)}, u32[]{:S(2)}) %collective-permute-start) | collective-permute-done | bytes 1048608 | tf_op jit(solution)/shard_map/while/body/eval_jaxpr/ppermute | solution.py:14
  297.2 1.7 fusion.25
  300.0 2.3 fusion.26
  302.7 5.9 %dynamic_update_slice.15 = f32[16,2,64,512]{3,2,0,1:T(8,128)} dynamic-update-slice(f32[16,2,64,512]{3,2,0,1:T(8,128)} %get-tuple-element.221, f32[16,2,64,64]{3,2,0,1:T(8,128)S(1)} %pad_maximum_fusion.4, s32[]{:T(128)} %constant.92.clone.1..sunk, s32[]{:T(128)} %constant.92.clone.1..sunk, s32[]{:T(128)} %constant.92.clone.1..sunk, s32[]{:T(128)S(6)} %select_n.84) | dynamic-update-slice | bytes 1048580 | tf_op jit(solution)/shard_map/while/body/eval_jaxpr/dynamic_update_slice | solution.py:50
  309.3 21.7 %collective-permute-done = bf16[16,2,64,256]{3,2,1,0:T(8,128)(2,1)S(1)} collective-permute-done((bf16[16,2,64,256]{3,2,1,0:T(8,128)(2,1)S(1)}, bf16[16,2,64,256]{3,2,1,0:T(8,128)(2,1)S(1)}, u32[]{:S(2)}, u32[]{:S(2)}) %collective-permute-start) | collective-permute-done | bytes 1048608 | tf_op jit(solution)/shard_map/while/body/eval_jaxpr/ppermute | solution.py:14
  331.9 1.7 fusion.25
  334.8 2.3 fusion.26
  337.4 8.9 %dynamic_update_slice.15 = f32[16,2,64,512]{3,2,0,1:T(8,128)} dynamic-update-slice(f32[16,2,64,512]{3,2,0,1:T(8,128)} %get-tuple-element.221, f32[16,2,64,64]{3,2,0,1:T(8,128)S(1)} %pad_maximum_fusion.4, s32[]{:T(128)} %constant.92.clone.1..sunk, s32[]{:T(128)} %constant.92.clone.1..sunk, s32[]{:T(128)} %constant.92.clone.1..sunk, s32[]{:T(128)S(6)} %select_n.84) | dynamic-update-slice | bytes 1048580 | tf_op jit(solution)/shard_map/while/body/eval_jaxpr/dynamic_update_slice | solution.py:50
  346.4 4.9 %copy.46 = f32[16,2,64,512]{3,2,1,0:T(8,128)} copy(f32[16,2,64,512]{3,2,0,1:T(8,128)} %get-tuple-element.138) | data formatting | bytes 8388608 | tf_op jit(solution)/shard_map/while | solution.py:83
  (75 shorter events, 22.3 us)
Async XLA Ops:
  26.5 18.8 %all-to-all-start = ((bf16[4,2,65536]{2,1,0:T(2,128)(2,1)}), bf16[4,2,65536]{2,1,0:T(2,128)(2,1)S(1)}, u32[]{:S(2)}, u32[]{:S(2)}) async-start(bf16[4,2,65536]{2,1,0:T(2,128)(2,1)} %reshape.341), calls=%async_computation | async-start | bytes 2097152 | tf_op jit(solution)/shard_map/all_to_all | solution.py:70
  71.0 30.3 %collective-permute-start = (bf16[16,2,64,256]{3,2,1,0:T(8,128)(2,1)S(1)}, bf16[16,2,64,256]{3,2,1,0:T(8,128)(2,1)S(1)}, u32[]{:S(2)}, u32[]{:S(2)}) collective-permute-start(bf16[16,2,64,256]{3,2,1,0:T(8,128)(2,1)S(1)} %get-tuple-element.220), channel_id=1, source_target_pairs={{28,0},{0,4},{4,8},{8,12},{12,16},{16,20},{20,24},{24,28},{29,1},{... | collective-permute-start | bytes 3145736 | tf_op jit(solution)/shard_map/while/body/eval_jaxpr/ppermute | solution.py:14
  101.4 1.0 copy-start
  107.5 8.4 %copy-start.1 = (bf16[16,2,64,256]{3,2,1,0:T(8,128)(2,1)S(1)}, bf16[16,2,64,256]{3,2,1,0:T(8,128)(2,1)}, u32[]{:S(2)}) copy-start(bf16[16,2,64,256]{3,2,1,0:T(8,128)(2,1)} %copy-done) | copy-start | bytes 3145732 | tf_op jit(solution)/shard_map/while
  116.0 26.9 %collective-permute-start = (bf16[16,2,64,256]{3,2,1,0:T(8,128)(2,1)S(1)}, bf16[16,2,64,256]{3,2,1,0:T(8,128)(2,1)S(1)}, u32[]{:S(2)}, u32[]{:S(2)}) collective-permute-start(bf16[16,2,64,256]{3,2,1,0:T(8,128)(2,1)S(1)} %get-tuple-element.220), channel_id=1, source_target_pairs={{28,0},{0,4},{4,8},{8,12},{12,16},{16,20},{20,24},{24,28},{29,1},{... | collective-permute-start | bytes 3145736 | tf_op jit(solution)/shard_map/while/body/eval_jaxpr/ppermute | solution.py:14
  142.9 1.0 copy-start
  149.0 5.6 %copy-start.1 = (bf16[16,2,64,256]{3,2,1,0:T(8,128)(2,1)S(1)}, bf16[16,2,64,256]{3,2,1,0:T(8,128)(2,1)}, u32[]{:S(2)}) copy-start(bf16[16,2,64,256]{3,2,1,0:T(8,128)(2,1)} %copy-done) | copy-start | bytes 3145732 | tf_op jit(solution)/shard_map/while
  154.7 25.9 %collective-permute-start = (bf16[16,2,64,256]{3,2,1,0:T(8,128)(2,1)S(1)}, bf16[16,2,64,256]{3,2,1,0:T(8,128)(2,1)S(1)}, u32[]{:S(2)}, u32[]{:S(2)}) collective-permute-start(bf16[16,2,64,256]{3,2,1,0:T(8,128)(2,1)S(1)} %get-tuple-element.220), channel_id=1, source_target_pairs={{28,0},{0,4},{4,8},{8,12},{12,16},{16,20},{20,24},{24,28},{29,1},{... | collective-permute-start | bytes 3145736 | tf_op jit(solution)/shard_map/while/body/eval_jaxpr/ppermute | solution.py:14
  180.6 1.0 copy-start
  186.8 9.2 %copy-start.1 = (bf16[16,2,64,256]{3,2,1,0:T(8,128)(2,1)S(1)}, bf16[16,2,64,256]{3,2,1,0:T(8,128)(2,1)}, u32[]{:S(2)}) copy-start(bf16[16,2,64,256]{3,2,1,0:T(8,128)(2,1)} %copy-done) | copy-start | bytes 3145732 | tf_op jit(solution)/shard_map/while
  196.0 25.0 %collective-permute-start = (bf16[16,2,64,256]{3,2,1,0:T(8,128)(2,1)S(1)}, bf16[16,2,64,256]{3,2,1,0:T(8,128)(2,1)S(1)}, u32[]{:S(2)}, u32[]{:S(2)}) collective-permute-start(bf16[16,2,64,256]{3,2,1,0:T(8,128)(2,1)S(1)} %get-tuple-element.220), channel_id=1, source_target_pairs={{28,0},{0,4},{4,8},{8,12},{12,16},{16,20},{20,24},{24,28},{29,1},{... | collective-permute-start | bytes 3145736 | tf_op jit(solution)/shard_map/while/body/eval_jaxpr/ppermute | solution.py:14
  221.1 1.0 copy-start
  227.2 6.3 %copy-start.1 = (bf16[16,2,64,256]{3,2,1,0:T(8,128)(2,1)S(1)}, bf16[16,2,64,256]{3,2,1,0:T(8,128)(2,1)}, u32[]{:S(2)}) copy-start(bf16[16,2,64,256]{3,2,1,0:T(8,128)(2,1)} %copy-done) | copy-start | bytes 3145732 | tf_op jit(solution)/shard_map/while
  233.6 24.1 %collective-permute-start = (bf16[16,2,64,256]{3,2,1,0:T(8,128)(2,1)S(1)}, bf16[16,2,64,256]{3,2,1,0:T(8,128)(2,1)S(1)}, u32[]{:S(2)}, u32[]{:S(2)}) collective-permute-start(bf16[16,2,64,256]{3,2,1,0:T(8,128)(2,1)S(1)} %get-tuple-element.220), channel_id=1, source_target_pairs={{28,0},{0,4},{4,8},{8,12},{12,16},{16,20},{20,24},{24,28},{29,1},{... | collective-permute-start | bytes 3145736 | tf_op jit(solution)/shard_map/while/body/eval_jaxpr/ppermute | solution.py:14
  257.7 1.0 copy-start
  263.8 9.2 %copy-start.1 = (bf16[16,2,64,256]{3,2,1,0:T(8,128)(2,1)S(1)}, bf16[16,2,64,256]{3,2,1,0:T(8,128)(2,1)}, u32[]{:S(2)}) copy-start(bf16[16,2,64,256]{3,2,1,0:T(8,128)(2,1)} %copy-done) | copy-start | bytes 3145732 | tf_op jit(solution)/shard_map/while
  273.1 23.2 %collective-permute-start = (bf16[16,2,64,256]{3,2,1,0:T(8,128)(2,1)S(1)}, bf16[16,2,64,256]{3,2,1,0:T(8,128)(2,1)S(1)}, u32[]{:S(2)}, u32[]{:S(2)}) collective-permute-start(bf16[16,2,64,256]{3,2,1,0:T(8,128)(2,1)S(1)} %get-tuple-element.220), channel_id=1, source_target_pairs={{28,0},{0,4},{4,8},{8,12},{12,16},{16,20},{20,24},{24,28},{29,1},{... | collective-permute-start | bytes 3145736 | tf_op jit(solution)/shard_map/while/body/eval_jaxpr/ppermute | solution.py:14
  296.2 1.0 copy-start
  302.4 6.2 %copy-start.1 = (bf16[16,2,64,256]{3,2,1,0:T(8,128)(2,1)S(1)}, bf16[16,2,64,256]{3,2,1,0:T(8,128)(2,1)}, u32[]{:S(2)}) copy-start(bf16[16,2,64,256]{3,2,1,0:T(8,128)(2,1)} %copy-done) | copy-start | bytes 3145732 | tf_op jit(solution)/shard_map/while
  308.7 22.2 %collective-permute-start = (bf16[16,2,64,256]{3,2,1,0:T(8,128)(2,1)S(1)}, bf16[16,2,64,256]{3,2,1,0:T(8,128)(2,1)S(1)}, u32[]{:S(2)}, u32[]{:S(2)}) collective-permute-start(bf16[16,2,64,256]{3,2,1,0:T(8,128)(2,1)S(1)} %get-tuple-element.220), channel_id=1, source_target_pairs={{28,0},{0,4},{4,8},{8,12},{12,16},{16,20},{20,24},{24,28},{29,1},{... | collective-permute-start | bytes 3145736 | tf_op jit(solution)/shard_map/while/body/eval_jaxpr/ppermute | solution.py:14
  331.0 1.0 copy-start
  337.1 9.2 %copy-start.1 = (bf16[16,2,64,256]{3,2,1,0:T(8,128)(2,1)S(1)}, bf16[16,2,64,256]{3,2,1,0:T(8,128)(2,1)}, u32[]{:S(2)}) copy-start(bf16[16,2,64,256]{3,2,1,0:T(8,128)(2,1)} %copy-done) | copy-start | bytes 3145732 | tf_op jit(solution)/shard_map/while
where the time goes:
time: 353 us; the launch traced here: 351 us
  waiting for transfers between devices  185 us (52%)
  local copies, waits for them, and re-layouts  118 us (33%)
  matrix products  19.2 us (5%)
  other arithmetic  16.9 us (5%)
  starting transfers between devices  11.1 us (3%)
    ppermute x7, waiting for transfers between devices, passed_along(): return lax.ppermute(block, axis, route)  171 us
    dynamic_update_slice x8, local copies, waits for them, and re-layouts, place_block(): return lax.dynamic_update_slice(result, block, (0, 0, 0, column_first))  57.6 us
    slice x8, local copies, waits for them, and re-layouts, cross_block(): real_part = products[:, 0, :, 0] + products[:, 1, :, 1]  18.7 us
    all_to_all x1, waiting for transfers between devices, per_device(): lax.all_to_all(weighted, 'freq', split_axis=0, concat_axis=3, tiled=True)  14.5 us
    dot_general x8, matrix products, cross_block(): jnp.einsum('fcw,fdw->fcd', own_panel.reshape(bin_count, 2 * row_count, wi...  13 us
    reshape x8, local copies, waits for them, and re-layouts, cross_block(): products = products.reshape(bin_count, 2, row_count, 2, col_count)  10.7 us
    convert_element_type x1, other arithmetic, per_device(): jnp.clip(strain.astype(jnp.float32), -limits, limits).astype(jnp.bfloat16)  10.6 us
    while x35, local copies, waits for them, and re-layouts  7.45 us
  transfers between devices with their start and end apart: 8, of which 8 were waited for; matrix products, arithmetic and copies ran while one was open for 0% of the time, Pallas kernels for 0%

commit v1 on v0

v1 whole, which is shorter than its diff:
```python
import functools
import math

import jax
import jax.numpy as jnp
from jax import lax
from jax.experimental import pallas as pl
from jax.experimental.pallas import tpu as pltpu
from jax.sharding import PartitionSpec as P

CLIP_FACTOR = 2.0
MESH = pl.DeviceIdType.MESH
PAIR = 2
BF16 = jnp.bfloat16
F32 = jnp.float32


def dft_rows(freq_bins, length):
    samples = jnp.arange(length, dtype=jnp.int32)
    phase_index = freq_bins[:, None] * samples[None, :] % length
    angle = phase_index.astype(F32) * (2.0 * math.pi / length)
    taper = 0.5 - 0.5 * jnp.cos(samples.astype(F32) * (2.0 * math.pi / length))
    cosine = taper[None, :] * jnp.cos(angle)
    sine = -taper[None, :] * jnp.sin(angle)
    return jnp.concatenate([cosine, sine], axis=0).astype(BF16)


def spectrum_kernel(limit_ref, count_ref, root_ref, table_ref, strain_ref, out_ref):
    block, wins, length = strain_ref.shape
    bins = out_ref.shape[1]
    first = pl.program_id(0) * block
    clipped = []
    for c in range(block):
        limit = jnp.full((wins, 128), limit_ref[first + c], F32).astype(BF16)
        limit = jnp.concatenate([limit] * (length // 128), axis=1)
        clipped.append(jnp.minimum(jnp.maximum(strain_ref[c], -limit), limit))
    rows = jnp.concatenate(clipped, axis=0)
    spectrum = lax.dot_general(
        table_ref[...], rows, (((1,), (1,)), ((), ())), preferred_element_type=F32
    )
    lane = lax.broadcasted_iota(jnp.int32, (bins, 2 * wins), 1)
    low = lane < wins
    window = lax.axis_index("freq") * wins + lax.rem(lane, wins)
    for c in range(0, block, 2):
        re = spectrum[:bins, c * wins : (c + 2) * wins]
        im = spectrum[bins:, c * wins : (c + 2) * wins]
        even = jnp.where(low, re, pltpu.roll(im, wins, 1))
        odd = jnp.where(low, pltpu.roll(re, wins, 1), im)
        for d, both in enumerate((even, odd)):
            channel = first + c + d
            weight = jnp.where(window < count_ref[channel], root_ref[channel], 0.0)
            out_ref[c + d] = (both * weight).astype(BF16)


def spectra(strain, limits, valid_count, roots, table):
    channels, wins, length = strain.shape
    bins = table.shape[0] // 2
    block = 8
    smem = pl.BlockSpec(memory_space=pltpu.SMEM)
    return pl.pallas_call(
        spectrum_kernel,
        grid=(channels // block,),
        out_shape=jax.ShapeDtypeStruct((channels, bins, 2 * wins), BF16),
        in_specs=[
            smem,
            smem,
            smem,
            pl.BlockSpec((2 * bins, length), lambda i: (0, 0)),
            pl.BlockSpec((block, wins, length), lambda i: (i, 0, 0)),
        ],
        out_specs=pl.BlockSpec((block, bins, 2 * wins), lambda i: (i, 0, 0)),
        compiler_params=pltpu.CompilerParams(vmem_limit_bytes=32 * 2**20),
    )(limits, valid_count, roots, table, strain)


def cross_kernel(groups, parts, w_ref, o_ref, panel, left, stage, own_sem, a_send, a_recv,
                 up_send, down_send, z_recv, r_send, r_recv):
    pieces = parts * PAIR
    bins, rows, lanes = panel.shape[2:]
    chan, q = lax.axis_index("chan"), lax.axis_index("freq")
    z, x = chan // PAIR, lax.rem(chan, PAIR)
    me = q * PAIR + x
    has_up, has_down = z < groups - 1, z > 0

    def place(piece):
        return (z * PAIR + lax.rem(piece, PAIR), piece // PAIR)

    above, below, mate = (chan + PAIR, q), (chan - PAIR, q), (z * PAIR + 1 - x, q)

    barrier = pltpu.get_barrier_semaphore()
    for d in range(1, pieces):
        pl.semaphore_signal(barrier, inc=1, device_id=place(lax.rem(me + d, pieces)), device_id_type=MESH)

    @pl.when(has_up)
    def _():
        pl.semaphore_signal(barrier, inc=1, device_id=above, device_id_type=MESH)

    @pl.when(has_down)
    def _():
        pl.semaphore_signal(barrier, inc=1, device_id=below, device_id_type=MESH)

    greeted = pieces - 1 + jnp.where(has_up, 1, 0) + jnp.where(has_down, 1, 0)
    pl.semaphore_wait(barrier, greeted)

    def swap(d):
        to = lax.rem(me + d, pieces)
        return pltpu.make_async_remote_copy(
            src_ref=w_ref.at[to], dst_ref=panel.at[z, me], send_sem=a_send.at[d],
            recv_sem=a_recv.at[d], device_id=place(to), device_id_type=MESH)

    def arrival(d):
        source = lax.rem(me + pieces - d, pieces)
        return source, pltpu.make_async_remote_copy(
            src_ref=w_ref.at[source], dst_ref=panel.at[z, source], send_sem=a_send.at[d],
            recv_sem=a_recv.at[d], device_id=place(source), device_id_type=MESH)

    def along(p, k, sems, target):
        return pltpu.make_async_remote_copy(
            src_ref=panel.at[p, k], dst_ref=panel.at[p, k], send_sem=sems.at[p, k],
            recv_sem=z_recv.at[p, k], device_id=target, device_id_type=MESH)

    def pass_up(p, k):
        @pl.when(has_up)
        def _():
            along(p, k, up_send, above).start()

    def pass_down(p, k):
        @pl.when(has_down)
        def _():
            along(p, k, down_send, below).start()

    own = pltpu.make_async_copy(w_ref.at[me], panel.at[z, me], own_sem)
    own.start()
    for d in range(1, pieces):
        swap(d).start()
    own.wait()
    pass_up(z, me)
    pass_down(z, me)
    for d in range(1, pieces):
        source, copy = arrival(d)
        copy.wait_recv()
        pass_up(z, source)
        pass_down(z, source)

    def wide(p, f):
        return jnp.concatenate(
            [
                jnp.concatenate([panel[p, part * PAIR + i, f] for i in range(PAIR)], axis=0)
                for part in range(parts)
            ],
            axis=1,
        )

    half = lanes // 2
    height = PAIR * rows

    @pl.loop(0, bins)
    def _(f):
        plain = wide(z, f)
        left[f, pl.ds(0, height)] = plain
        sign = jnp.where(lax.broadcasted_iota(jnp.int32, (height, lanes), 1) < half, 1.0, -1.0)
        for part in range(parts):
            turned = pltpu.roll(plain[:, part * lanes : (part + 1) * lanes].astype(F32), half, 1)
            left[f, pl.ds(height, height), pl.ds(part * lanes, lanes)] = (turned * sign).astype(BF16)

    def give_back(p):
        return pltpu.make_async_remote_copy(
            src_ref=stage.at[p],
            dst_ref=o_ref.at[pl.ds(x * bins, bins), :, :, pl.ds(pl.multiple_of(p * height, height), height)],
            send_sem=r_send.at[p], recv_sem=r_recv.at[p], device_id=mate, device_id_type=MESH)

    def get_back(p):
        return pltpu.make_async_remote_copy(
            src_ref=stage.at[p],
            dst_ref=o_ref.at[pl.ds((1 - x) * bins, bins), :, :, pl.ds(pl.multiple_of(p * height, height), height)],
            send_sem=r_send.at[p], recv_sem=r_recv.at[p], device_id=mate, device_id_type=MESH)

    def block(p):
        columns = pl.ds(pl.multiple_of(p * height, height), height)

        @pl.loop(0, bins)
        def _(f):
            product = lax.dot_general(
                left[f], wide(p, f), (((1,), (1,)), ((), ())), preferred_element_type=F32
            ).astype(BF16)
            for part in range(2):
                lower = product[part * height : part * height + rows]
                upper = product[part * height + rows : (part + 1) * height]
                first = x == 0
                o_ref[x * bins + f, part, :, columns] = jnp.where(first, lower, upper)
                stage[p, f, part] = jnp.where(first, upper, lower)

        give_back(p).start()

    block(z)

    def step(s, carry):
        lower, upper = z - 1 - s, z + 1 + s
        for k in range(pieces):
            @pl.when(lower >= 0)
            def _():
                along(lower, k, up_send, above).wait_recv()
                pass_up(lower, k)

            @pl.when(upper < groups)
            def _():
                along(upper, k, down_send, below).wait_recv()
                pass_down(upper, k)

        @pl.when(lower >= 0)
        def _():
            block(lower)

        @pl.when(upper < groups)
        def _():
            block(upper)

        return carry

    lax.fori_loop(0, groups - 1, step, 0)

    for d in range(1, pieces):
        swap(d).wait_send()

    def finish(p, carry):
        give_back(p).wait_send()
        get_back(p).wait_recv()
        for k in range(pieces):
            @pl.when(has_up & (p <= z))
            def _():
                along(p, k, up_send, above).wait_send()

            @pl.when(has_down & (p >= z))
            def _():
                along(p, k, down_send, below).wait_send()

        return carry

    lax.fori_loop(0, groups, finish, 0)


def cross(weighted, groups, parts):
    pieces, bins, rows, lanes = weighted.shape
    dma = pltpu.SemaphoreType.DMA
    return pl.pallas_call(
        functools.partial(cross_kernel, groups, parts),
        out_shape=jax.ShapeDtypeStruct((PAIR * bins, 2, rows, groups * PAIR * rows), BF16),
        in_specs=[pl.BlockSpec(memory_space=pl.ANY)],
        out_specs=pl.BlockSpec(memory_space=pltpu.VMEM),
        scratch_shapes=[
            pltpu.VMEM((groups, pieces, bins, rows, lanes), BF16),
            pltpu.VMEM((bins, 2 * PAIR * rows, parts * lanes), BF16),
            pltpu.VMEM((groups, bins, 2, rows, PAIR * rows), BF16),
            dma, dma((pieces,)), dma((pieces,)),
            dma((groups, pieces)), dma((groups, pieces)), dma((groups, pieces)),
            dma((groups,)), dma((groups,)),
        ],
        compiler_params=pltpu.CompilerParams(
            collective_id=0, has_side_effects=True, vmem_limit_bytes=56 * 2**20
        ),
    )(weighted)


def per_device(strain, mad_index, mad_table, freq_bins, valid_count):
    channels, wins, length = strain.shape
    bins = freq_bins.shape[0]
    entries = jnp.arange(mad_table.shape[0], dtype=jnp.int32)
    matches = mad_index[:, None] == entries[None, :]
    limits = jnp.sum(jnp.where(matches, mad_table[None, :], 0.0), axis=1) * CLIP_FACTOR
    roots = 1.0 / jnp.sqrt(valid_count.astype(F32))
    table = dft_rows(freq_bins, length)
    weighted = spectra(strain, limits, valid_count, roots, table)
    parts, groups = lax.axis_size("freq"), lax.axis_size("chan") // PAIR
    pieces = parts * PAIR
    weighted = jnp.transpose(weighted, (1, 0, 2)).reshape(pieces, bins // pieces, channels, 2 * wins)
    return cross(weighted, groups, parts).astype(F32)


def solution(mesh):
    return jax.shard_map(
        per_device,
        mesh=mesh,
        in_specs=(P("chan", "freq", None), P("chan"), P(), P(), P("chan")),
        out_specs=P("freq", None, "chan", None),
        check_vma=False,
    )
```

time: 353 us -> 105 us (0.30)
  waiting for transfers between devices: 185 us -> 0 us
  local copies, waits for them, and re-layouts: 118 us -> 5.68 us
  Pallas kernels: 0 us -> 91.3 us
  matrix products: 19.2 us -> 0 us
  starting transfers between devices: 11.1 us -> 0 us
  other arithmetic: 16.9 us -> 7.56 us
    ppermute x7 -> x0, waiting for transfers between devices: 171 us -> none  [passed_along(): return lax.ppermute(block, axis, route)]
    pallas_call x0 -> x2, Pallas kernels: none -> 91.3 us  [the longest x1 85.9 us: cross(): pl.pallas_call(functools.partial(cross_kernel, groups, parts), out_shape=...]
    dynamic_update_slice x8 -> x0, local copies, waits for them, and re-layouts: 57.6 us -> none  [place_block(): return lax.dynamic_update_slice(result, block, (0, 0, 0, column_first))]
    dot_general x9 -> x0, matrix products: 19.2 us -> none  [the longest x8 13 us: cross_block(): jnp.einsum('fcw,fdw->fcd', own_panel.reshape(bin_count, 2 * row_count, wi...]
    slice x8 -> x0, local copies, waits for them, and re-layouts: 18.7 us -> none  [cross_block(): real_part = products[:, 0, :, 0] + products[:, 1, :, 1]]
    all_to_all x1 -> x0, waiting for transfers between devices: 14.5 us -> none  [per_device(): lax.all_to_all(weighted, 'freq', split_axis=0, concat_axis=3, tiled=True)]
    reshape x10 -> x0, local copies, waits for them, and re-layouts: 14.3 us -> none  [the longest x8 10.7 us: cross_block(): products = products.reshape(bin_count, 2, row_count, 2, col_count)]
    while x36 -> x0, local copies, waits for them, and re-layouts: 12.4 us -> none
  transfers between devices with their start and end apart: 8 -> 0, of which waited for: 8 -> 0; matrix products, arithmetic and copies ran while one was open for 0% -> 0% of each run, Pallas kernels for 0% -> 0%
where the time goes in v1:
time: 105 us
  Pallas kernels  91.3 us (87%)
  other arithmetic  7.56 us (7%)
  local copies, waits for them, and re-layouts  5.68 us (5%)
    pallas_call x1, Pallas kernels, cross(): pl.pallas_call(functools.partial(cross_kernel, groups, parts), out_shape=...  85.9 us
    pallas_call x1, Pallas kernels, spectra(): pl.pallas_call(spectrum_kernel, grid=(channels // block,), out_shape=jax....  5.44 us
    convert_element_type x1, other arithmetic, per_device(): return cross(weighted, groups, parts).astype(F32)  4.17 us
    unnamed x4, local copies, waits for them, and re-layouts  4.03 us

profile of v1, /device:TPU:0, one launch (start us, length us, event | category | flops | bytes accessed | tf_op | source)
XLA Modules:
  0.0 104.6 jit_solution(18415906460223036171)
XLA Ops:
  0.0 0.8 select_reduce_fusion
  0.8 0.7 convert_rsqrt_fusion
  1.5 1.9 %multiply_convert_fusion.1 = (bf16[64,1024]{1,0:T(8,128)(2,1)S(1)}, bf16[64,1024]{1,0:T(8,128)(2,1)S(1)}) fusion(s32[64]{0:T(128)} %param.8, f32[1024]{0:T(1024)S(1)} %get-tuple-element.7, f32[1024]{0:T(1024)S(1)} %get-tuple-element.8), kind=kLoop, calls=%fused_computation.8 | loop fusion | flops 1179648 | bytes 270592 | tf_op jit(solution)/shard_map/convert
  3.4 0.0 copy-start
  3.4 3.4 %copy-done = bf16[64,64,1024]{2,1,0:T(8,128)(2,1)S(1)} copy-done((bf16[64,64,1024]{2,1,0:T(8,128)(2,1)S(1)}, bf16[64,64,1024]{2,1,0:T(8,128)(2,1)}, u32[]{:S(2)}) %copy-start) | copy-done | bytes 8388632
  6.8 0.0 copy-start.1
  6.8 0.7 copy-done.1
  7.5 5.4 %shard_map.55 = bf16[64,64,128]{2,1,0:T(8,128)(2,1)S(1)} custom-call(f32[64]{0:T(128)S(1)} %get-tuple-element.10.limit_ref, s32[64]{0:T(128)S(1)} %copy-done.1, f32[64]{0:T(128)S(1)} %get-tuple-element.9.root_ref, bf16[128,1024]{1,0:T(8,128)(2,1)S(1)} %pad_maximum_fusion.table_ref, bf16[64,64,1024]{2,1,0:T(8,128)(2,1)S(1)} %copy-done), custom_call_target="tpu_custom_call" | custom-call | tf_op jit(solution)/shard_map/pallas_call | solution.py:60
  12.9 1.6 %copy.7 = bf16[64,64,128]{2,1,0:T(8,128)(2,1)} copy(bf16[64,64,128]{2,0,1:T(8,128)(2,1)S(1)} %bitcast.2) | data formatting | bytes 2097152 | tf_op jit(solution)/shard_map/transpose | solution.py:275
  14.6 85.9 %shard_map.56 = bf16[16,2,64,512]{3,2,1,0:T(8,128)(2,1)} custom-call(bf16[8,8,64,128]{3,2,1,0:T(8,128)(2,1)} %bitcast.3), custom_call_target="tpu_custom_call" | custom-call | tf_op jit(solution)/shard_map/pallas_call | solution.py:245
  100.5 4.2 %convert_element_type.25 = f32[16,2,64,512]{3,2,1,0:T(8,128)} convert(bf16[16,2,64,512]{3,2,1,0:T(8,128)(2,1)} %shard_map.56) | non-fusion elementwise | flops 1048576 | bytes 6291456 | tf_op jit(solution)/shard_map/convert_element_type | solution.py:276
  (2 shorter events, 0.1 us)
Async XLA Ops:
  3.4 3.4 %copy-start = (bf16[64,64,1024]{2,1,0:T(8,128)(2,1)S(1)}, bf16[64,64,1024]{2,1,0:T(8,128)(2,1)}, u32[]{:S(2)}) copy-start(bf16[64,64,1024]{2,1,0:T(8,128)(2,1)} %strain_ref.1) | copy-start | bytes 25165828
  6.8 0.7 copy-start.1

commit v2 on v1

v2 whole, which is shorter than its diff:
```python
import functools
import math

import jax
import jax.numpy as jnp
from jax import lax
from jax.experimental import pallas as pl
from jax.experimental.pallas import tpu as pltpu
from jax.sharding import PartitionSpec as P

CLIP_FACTOR = 2.0
MESH = pl.DeviceIdType.MESH
PAIR = 2
BF16 = jnp.bfloat16
F32 = jnp.float32


def dft_rows(freq_bins, length):
    samples = jnp.arange(length, dtype=jnp.int32)
    phase_index = freq_bins[:, None] * samples[None, :] % length
    angle = phase_index.astype(F32) * (2.0 * math.pi / length)
    taper = 0.5 - 0.5 * jnp.cos(samples.astype(F32) * (2.0 * math.pi / length))
    cosine = taper[None, :] * jnp.cos(angle)
    sine = -taper[None, :] * jnp.sin(angle)
    return jnp.concatenate([cosine, sine], axis=0).astype(BF16)


def spectrum_kernel(limit_ref, count_ref, root_ref, table_ref, strain_ref, out_ref):
    block, wins, length = strain_ref.shape
    bins = out_ref.shape[1]
    first = pl.program_id(0) * block
    clipped = []
    for c in range(block):
        limit = jnp.full((wins, 128), limit_ref[first + c], F32).astype(BF16)
        limit = jnp.concatenate([limit] * (length // 128), axis=1)
        clipped.append(jnp.minimum(jnp.maximum(strain_ref[c], -limit), limit))
    rows = jnp.concatenate(clipped, axis=0)
    spectrum = lax.dot_general(
        table_ref[...], rows, (((1,), (1,)), ((), ())), preferred_element_type=F32
    )
    lane = lax.broadcasted_iota(jnp.int32, (bins, 2 * wins), 1)
    low = lane < wins
    window = lax.axis_index("freq") * wins + lax.rem(lane, wins)
    for c in range(0, block, 2):
        re = spectrum[:bins, c * wins : (c + 2) * wins]
        im = spectrum[bins:, c * wins : (c + 2) * wins]
        even = jnp.where(low, re, pltpu.roll(im, wins, 1))
        odd = jnp.where(low, pltpu.roll(re, wins, 1), im)
        for d, both in enumerate((even, odd)):
            channel = first + c + d
            weight = jnp.where(window < count_ref[channel], root_ref[channel], 0.0)
            out_ref[c + d] = (both * weight).astype(BF16)


def spectra(strain, limits, valid_count, roots, table):
    channels, wins, length = strain.shape
    bins = table.shape[0] // 2
    block = 8
    smem = pl.BlockSpec(memory_space=pltpu.SMEM)
    return pl.pallas_call(
        spectrum_kernel,
        grid=(channels // block,),
        out_shape=jax.ShapeDtypeStruct((channels, bins, 2 * wins), BF16),
        in_specs=[
            smem,
            smem,
            smem,
            pl.BlockSpec((2 * bins, length), lambda i: (0, 0)),
            pl.BlockSpec((block, wins, length), lambda i: (i, 0, 0)),
        ],
        out_specs=pl.BlockSpec((block, bins, 2 * wins), lambda i: (i, 0, 0)),
        compiler_params=pltpu.CompilerParams(vmem_limit_bytes=60 * 2**20),
    )(limits, valid_count, roots, table, strain)


def cross_kernel(groups, parts, cuts, w_ref, o_ref, panel, left, left_end, stage, stage_end, own_sem, a_send,
                 a_recv, up_send, down_send, z_recv, r_send, r_recv, e_send, e_recv):
    pieces = parts * PAIR
    bins, rows, lanes = panel.shape[2:]
    cut = bins // cuts
    height = PAIR * rows
    half = lanes // 2
    last = groups - 1
    chan, q = lax.axis_index("chan"), lax.axis_index("freq")
    z, x = chan // PAIR, lax.rem(chan, PAIR)
    me = q * PAIR + x
    is_end = (z == 0) | (z == last)
    is_inner = (z > 0) & (z < last)
    low_pair, high_pair = (z == 1), (z == last - 1)
    is_helper = low_pair | high_pair
    end = jnp.where(low_pair, 0, last)
    sends_up, sends_down = z < last - 1, z > 1

    def place(piece):
        return (z * PAIR + lax.rem(piece, PAIR), piece // PAIR)

    def at(group, side):
        return (group * PAIR + side, q)

    above, below, mate = at(z + 1, x), at(z - 1, x), at(z, 1 - x)

    barrier = pltpu.get_barrier_semaphore()

    def greet(device):
        pl.semaphore_signal(barrier, inc=1, device_id=device, device_id_type=MESH)

    for d in range(1, pieces):
        greet(place(lax.rem(me + d, pieces)))

    @pl.when(z < last)
    def _():
        greet(above)

    @pl.when(z > 0)
    def _():
        greet(below)

    @pl.when((z == 0) | high_pair)
    def _():
        greet(at(z + 1, 1 - x))

    @pl.when((z == last) | low_pair)
    def _():
        greet(at(z - 1, 1 - x))

    greeted = pieces - 1 + jnp.where(z < last, 1, 0) + jnp.where(z > 0, 1, 0)
    greeted = greeted + jnp.where(is_end | is_helper, 1, 0)
    pl.semaphore_wait(barrier, greeted)

    def span(h):
        return pl.ds(h * cut, cut)

    def swap(d, h):
        to = lax.rem(me + d, pieces)
        return pltpu.make_async_remote_copy(
            src_ref=w_ref.at[to, span(h)], dst_ref=panel.at[z, me, span(h)], send_sem=a_send.at[d, h],
            recv_sem=a_recv.at[d, h], device_id=place(to), device_id_type=MESH)

    def arrival(d, h):
        source = lax.rem(me + pieces - d, pieces)
        return source, pltpu.make_async_remote_copy(
            src_ref=w_ref.at[source, span(h)], dst_ref=panel.at[z, source, span(h)], send_sem=a_send.at[d, h],
            recv_sem=a_recv.at[d, h], device_id=place(source), device_id_type=MESH)

    def along(p, k, h, sems, target):
        return pltpu.make_async_remote_copy(
            src_ref=panel.at[p, k, span(h)], dst_ref=panel.at[p, k, span(h)], send_sem=sems.at[p, k, h],
            recv_sem=z_recv.at[p, k, h], device_id=target, device_id_type=MESH)

    def pass_up(p, k, h):
        @pl.when(sends_up)
        def _():
            along(p, k, h, up_send, above).start()

    def pass_down(p, k, h):
        @pl.when(sends_down)
        def _():
            along(p, k, h, down_send, below).start()

    own = pltpu.make_async_copy(w_ref.at[me], panel.at[z, me], own_sem)
    own.start()
    for h in range(cuts):
        for d in range(1, pieces):
            swap(d, h).start()
    own.wait()

    def wide(p, f):
        return jnp.concatenate(
            [
                jnp.concatenate([panel[p, part * PAIR + i, f] for i in range(PAIR)], axis=0)
                for part in range(parts)
            ],
            axis=1,
        )

    def make_left(target, p, h):
        @pl.loop(0, cut)
        def _(i):
            f = h * cut + i
            plain = wide(p, f)
            target[f, pl.ds(0, height)] = plain
            sign = jnp.where(lax.broadcasted_iota(jnp.int32, (height, lanes), 1) < half, 1.0, -1.0)
            for part in range(parts):
                turned = pltpu.roll(plain[:, part * lanes : (part + 1) * lanes].astype(F32), half, 1)
                target[f, pl.ds(height, height), pl.ds(part * lanes, lanes)] = (turned * sign).astype(BF16)

    def columns(p):
        return pl.ds(pl.multiple_of(p * height, height), height)

    def give_back(p, h, side):
        return pltpu.make_async_remote_copy(
            src_ref=stage.at[p, span(h)],
            dst_ref=o_ref.at[pl.ds(side * bins + h * cut, cut), :, :, columns(p)],
            send_sem=r_send.at[p, h], recv_sem=r_recv.at[p, h], device_id=mate, device_id_type=MESH)

    def give_end(p, h, to, source):
        return pltpu.make_async_remote_copy(
            src_ref=stage_end.at[p, to, span(h)],
            dst_ref=o_ref.at[pl.ds(source * bins + h * cut, cut), :, :, columns(p)],
            send_sem=e_send.at[p, to, h], recv_sem=e_recv.at[p, source, h],
            device_id=at(end, to), device_id_type=MESH)

    def product_of(lhs, p, f):
        return lax.dot_general(
            lhs[f], wide(p, f), (((1,), (1,)), ((), ())), preferred_element_type=F32
        ).astype(BF16)

    def block(p, h):
        @pl.loop(0, cut)
        def _(i):
            f = h * cut + i
            product = product_of(left, p, f)
            for part in range(2):
                lower = product[part * height : part * height + rows]
                upper = product[part * height + rows : (part + 1) * height]
                o_ref[x * bins + f, part, :, columns(p)] = jnp.where(x == 0, lower, upper)
                stage[p, f, part] = jnp.where(x == 0, upper, lower)

        give_back(p, h, x).start()

    def block_end(p, h):
        @pl.loop(0, cut)
        def _(i):
            f = h * cut + i
            product = product_of(left_end, p, f)
            for part in range(2):
                for to in range(PAIR):
                    top = part * height + to * rows
                    stage_end[p, to, f, part] = product[top : top + rows]

        for to in range(PAIR):
            give_end(p, h, to, x).start()

    for h in range(cuts):
        pass_up(z, me, h)
        pass_down(z, me, h)
    for h in range(cuts):
        for d in range(1, pieces):
            source, copy = arrival(d, h)
            copy.wait_recv()
            pass_up(z, source, h)
            pass_down(z, source, h)
    for h in range(cuts):
        make_left(left, z, h)
        block(z, h)

    def step(s, carry):
        lower, upper = z - 1 - s, z + 1 + s
        for h in range(cuts):
            @pl.when(lower >= 0)
            def _():
                for k in range(pieces):
                    along(lower, k, h, up_send, above).wait_recv()
                    pass_up(lower, k, h)

            @pl.when(upper <= last)
            def _():
                for k in range(pieces):
                    along(upper, k, h, down_send, below).wait_recv()
                    pass_down(upper, k, h)

            @pl.when(is_helper & (s == 0))
            def _():
                make_left(left_end, end, h)
                block_end(z, h)

            @pl.when(is_helper & (lower > 0))
            def _():
                block_end(lower, h)

            @pl.when(is_helper & (upper < last))
            def _():
                block_end(upper, h)

            @pl.when(low_pair & (upper == last))
            def _():
                block_end(upper, h)

            @pl.when(high_pair & (lower == 0))
            def _():
                block_end(lower, h)

            @pl.when(lower >= 0)
            def _():
                block(lower, h)

            @pl.when(upper <= last)
            def _():
                block(upper, h)

        return carry

    @pl.when(is_inner)
    def _():
        lax.fori_loop(0, last, step, 0)

    for h in range(cuts):
        for d in range(1, pieces):
            swap(d, h).wait_send()

    def finish(p, carry):
        for h in range(cuts):
            @pl.when(is_inner | (p == z))
            def _():
                give_back(p, h, x).wait_send()
                give_back(p, h, 1 - x).wait_recv()

            @pl.when(is_end & (p != z))
            def _():
                for source in range(PAIR):
                    give_end(p, h, 0, source).wait_recv()

            @pl.when(is_helper & (p != end))
            def _():
                for to in range(PAIR):
                    give_end(p, h, to, x).wait_send()

            for k in range(pieces):
                @pl.when(sends_up & (p <= z))
                def _():
                    along(p, k, h, up_send, above).wait_send()

                @pl.when(sends_down & (p >= z))
                def _():
                    along(p, k, h, down_send, below).wait_send()

        return carry

    lax.fori_loop(0, groups, finish, 0)


def cross(weighted, groups, parts):
    assert groups >= 4
    pieces, bins, rows, lanes = weighted.shape
    cuts = 2
    dma = pltpu.SemaphoreType.DMA
    left = pltpu.VMEM((bins, 2 * PAIR * rows, parts * lanes), BF16)
    return pl.pallas_call(
        functools.partial(cross_kernel, groups, parts, cuts),
        out_shape=jax.ShapeDtypeStruct((PAIR * bins, 2, rows, groups * PAIR * rows), BF16),
        in_specs=[pl.BlockSpec(memory_space=pl.ANY)],
        out_specs=pl.BlockSpec(memory_space=pltpu.VMEM),
        scratch_shapes=[
            pltpu.VMEM((groups, pieces, bins, rows, lanes), BF16),
            left,
            left,
            pltpu.VMEM((groups, bins, 2, rows, PAIR * rows), BF16),
            pltpu.VMEM((groups, PAIR, bins, 2, rows, PAIR * rows), BF16),
            dma, dma((pieces, cuts)), dma((pieces, cuts)),
            dma((groups, pieces, cuts)), dma((groups, pieces, cuts)), dma((groups, pieces, cuts)),
            dma((groups, cuts)), dma((groups, cuts)),
            dma((groups, PAIR, cuts)), dma((groups, PAIR, cuts)),
        ],
        compiler_params=pltpu.CompilerParams(
            collective_id=0, has_side_effects=True, vmem_limit_bytes=56 * 2**20
        ),
    )(weighted)


def per_device(strain, mad_index, mad_table, freq_bins, valid_count):
    channels, wins, length = strain.shape
    bins = freq_bins.shape[0]
    entries = jnp.arange(mad_table.shape[0], dtype=jnp.int32)
    matches = mad_index[:, None] == entries[None, :]
    limits = jnp.sum(jnp.where(matches, mad_table[None, :], 0.0), axis=1) * CLIP_FACTOR
    roots = 1.0 / jnp.sqrt(valid_count.astype(F32))
    table = dft_rows(freq_bins, length)
    weighted = spectra(strain, limits, valid_count, roots, table)
    parts, groups = lax.axis_size("freq"), lax.axis_size("chan") // PAIR
    pieces = parts * PAIR
    weighted = jnp.transpose(weighted, (1, 0, 2)).reshape(pieces, bins // pieces, channels, 2 * wins)
    return cross(weighted, groups, parts).astype(F32)


def solution(mesh):
    return jax.shard_map(
        per_device,
        mesh=mesh,
        in_specs=(P("chan", "freq", None), P("chan"), P(), P(), P("chan")),
        out_specs=P("freq", None, "chan", None),
        check_vma=False,
    )
```

time: 105 us -> 84.9 us (0.81)
  Pallas kernels: 91.3 us -> 72.1 us
  local copies, waits for them, and re-layouts: 5.68 us -> 2.9 us
  other arithmetic: 7.56 us -> 8.79 us
    pallas_call x1, Pallas kernels: 85.9 us -> 63 us  [cross(): pl.pallas_call(functools.partial(cross_kernel, groups, parts, cuts), out_...]
    unnamed x4 -> x0, local copies, waits for them, and re-layouts: 4.03 us -> none
    pallas_call x1, Pallas kernels: 5.44 us -> 9.07 us  [spectra(): pl.pallas_call(spectrum_kernel, grid=(channels // block,), out_shape=jax....]
    transpose x1, local copies, waits for them, and re-layouts: 1.65 us -> 2.9 us  [per_device(): jnp.transpose(weighted, (1, 0, 2))]
where the time goes in v2:
time: 84.9 us; the launch traced here: 83.8 us
  Pallas kernels  72.1 us (85%)
  other arithmetic  8.79 us (10%)
  local copies, waits for them, and re-layouts  2.9 us (3%)
    pallas_call x1, Pallas kernels, cross(): pl.pallas_call(functools.partial(cross_kernel, groups, parts, cuts), out_...  63 us
    pallas_call x1, Pallas kernels, spectra(): pl.pallas_call(spectrum_kernel, grid=(channels // block,), out_shape=jax....  9.07 us
    convert_element_type x1, other arithmetic, per_device(): return cross(weighted, groups, parts).astype(F32)  4.17 us
    transpose x1, local copies, waits for them, and re-layouts, per_device(): jnp.transpose(weighted, (1, 0, 2))  2.9 us
    another operation x1, other arithmetic  1.91 us

profile of v2, /device:TPU:0, one launch (start us, length us, event | category | flops | bytes accessed | tf_op | source)
XLA Modules:
  0.0 83.8 jit_solution(16188375778072269489)
XLA Ops:
  0.0 0.8 select_reduce_fusion
  0.8 1.2 %convert_rsqrt_fusion = (f32[64]{0:T(128)}, f32[64]{0:T(128)}) fusion(s32[64]{0:T(128)} %count_ref.1, f32[64]{0:T(128)S(1)} %select_reduce_fusion), kind=kLoop, calls=%fused_computation.16 | loop fusion | flops 128 | bytes 1024 | tf_op jit(solution)/shard_map/sqrt | solution.py:366
  2.0 1.9 %multiply_convert_fusion.1 = (bf16[64,1024]{1,0:T(8,128)(2,1)S(1)}, bf16[64,1024]{1,0:T(8,128)(2,1)S(1)}) fusion(s32[64]{0:T(128)} %param.8, f32[1024]{0:T(1024)S(1)} %get-tuple-element.7, f32[1024]{0:T(1024)S(1)} %get-tuple-element.8), kind=kLoop, calls=%fused_computation.8 | loop fusion | flops 1179648 | bytes 270592 | tf_op jit(solution)/shard_map/convert
  3.9 0.7 pad_maximum_fusion.table_ref
  4.6 9.1 %shard_map.55 = bf16[64,64,128]{2,1,0:T(8,128)(2,1)} custom-call(f32[64]{0:T(128)} %get-tuple-element.10.limit_ref, s32[64]{0:T(128)} %count_ref.1, f32[64]{0:T(128)} %get-tuple-element.9.root_ref, bf16[128,1024]{1,0:T(8,128)(2,1)} %pad_maximum_fusion.table_ref, bf16[64,64,1024]{2,1,0:T(8,128)(2,1)} %strain_ref.1), custom_call_target="tpu_custom_call" | custom-call | tf_op jit(solution)/shard_map/pallas_call | solution.py:60
  13.7 2.9 %copy.7 = bf16[64,64,128]{2,1,0:T(8,128)(2,1)} copy(bf16[64,64,128]{2,0,1:T(8,128)(2,1)} %bitcast.2) | data formatting | bytes 2097152 | tf_op jit(solution)/shard_map/transpose | solution.py:371
  16.6 63.0 %shard_map.56 = bf16[16,2,64,512]{3,2,1,0:T(8,128)(2,1)} custom-call(bf16[8,8,64,128]{3,2,1,0:T(8,128)(2,1)} %bitcast.3), custom_call_target="tpu_custom_call" | custom-call | tf_op jit(solution)/shard_map/pallas_call | solution.py:338
  79.6 4.2 %convert_element_type.25 = f32[16,2,64,512]{3,2,1,0:T(8,128)} convert(bf16[16,2,64,512]{3,2,1,0:T(8,128)(2,1)} %shard_map.56) | non-fusion elementwise | flops 1048576 | bytes 6291456 | tf_op jit(solution)/shard_map/convert_element_type | solution.py:372
  (1 shorter events, 0.0 us)

commit v3 on v2

--- a/solution.py
+++ b/solution.py
@@ -27,7 +27,7 @@
 
 def spectrum_kernel(limit_ref, count_ref, root_ref, table_ref, strain_ref, out_ref):
     block, wins, length = strain_ref.shape
-    bins = out_ref.shape[1]
+    bins = out_ref.shape[0]
     first = pl.program_id(0) * block
     clipped = []
     for c in range(block):
@@ -41,6 +41,7 @@
     lane = lax.broadcasted_iota(jnp.int32, (bins, 2 * wins), 1)
     low = lane < wins
     window = lax.axis_index("freq") * wins + lax.rem(lane, wins)
+    weighted = []
     for c in range(0, block, 2):
         re = spectrum[:bins, c * wins : (c + 2) * wins]
         im = spectrum[bins:, c * wins : (c + 2) * wins]
@@ -49,18 +50,19 @@
         for d, both in enumerate((even, odd)):
             channel = first + c + d
             weight = jnp.where(window < count_ref[channel], root_ref[channel], 0.0)
-            out_ref[c + d] = (both * weight).astype(BF16)
+            weighted.append(both * weight)
+    out_ref[...] = jnp.swapaxes(jnp.stack(weighted), 0, 1).astype(BF16)
 
 
 def spectra(strain, limits, valid_count, roots, table):
     channels, wins, length = strain.shape
     bins = table.shape[0] // 2
-    block = 8
+    block = 16
     smem = pl.BlockSpec(memory_space=pltpu.SMEM)
     return pl.pallas_call(
         spectrum_kernel,
         grid=(channels // block,),
-        out_shape=jax.ShapeDtypeStruct((channels, bins, 2 * wins), BF16),
+        out_shape=jax.ShapeDtypeStruct((bins, channels, 2 * wins), BF16),
         in_specs=[
             smem,
             smem,
@@ -68,8 +70,8 @@
             pl.BlockSpec((2 * bins, length), lambda i: (0, 0)),
             pl.BlockSpec((block, wins, length), lambda i: (i, 0, 0)),
         ],
-        out_specs=pl.BlockSpec((block, bins, 2 * wins), lambda i: (i, 0, 0)),
-        compiler_params=pltpu.CompilerParams(vmem_limit_bytes=60 * 2**20),
+        out_specs=pl.BlockSpec((bins, block, 2 * wins), lambda i: (0, i, 0)),
+        compiler_params=pltpu.CompilerParams(vmem_limit_bytes=32 * 2**20),
     )(limits, valid_count, roots, table, strain)
 
 
@@ -332,7 +334,7 @@
 def cross(weighted, groups, parts):
     assert groups >= 4
     pieces, bins, rows, lanes = weighted.shape
-    cuts = 2
+    cuts = 4
     dma = pltpu.SemaphoreType.DMA
     left = pltpu.VMEM((bins, 2 * PAIR * rows, parts * lanes), BF16)
     return pl.pallas_call(
@@ -368,7 +370,7 @@
     weighted = spectra(strain, limits, valid_count, roots, table)
     parts, groups = lax.axis_size("freq"), lax.axis_size("chan") // PAIR
     pieces = parts * PAIR
-    weighted = jnp.transpose(weighted, (1, 0, 2)).reshape(pieces, bins // pieces, channels, 2 * wins)
+    weighted = weighted.reshape(pieces, bins // pieces, channels, 2 * wins)
     return cross(weighted, groups, parts).astype(F32)
 
 

time: 84.9 us -> 80.6 us (0.949); the launches traced: 83.8 us -> 80.4 us
  Pallas kernels: 72.1 us -> 67.8 us
  local copies, waits for them, and re-layouts: 2.9 us -> 5 us
  other arithmetic: 8.79 us -> 7.56 us
    unnamed x0 -> x6, local copies, waits for them, and re-layouts: none -> 5 us
    pallas_call x1, Pallas kernels: 9.07 us -> 4.67 us  [spectra(): pl.pallas_call(spectrum_kernel, grid=(channels // block,), out_shape=jax....]
    transpose x1 -> x0, local copies, waits for them, and re-layouts: 2.9 us -> none  [per_device(): jnp.transpose(weighted, (1, 0, 2))]
where the time goes in v3:
time: 80.6 us; the launch traced here: 80.4 us
  Pallas kernels  67.8 us (84%)
  other arithmetic  7.56 us (9%)
  local copies, waits for them, and re-layouts  5 us (6%)
    pallas_call x1, Pallas kernels, cross(): pl.pallas_call(functools.partial(cross_kernel, groups, parts, cuts), out_...  63.1 us
    unnamed x6, local copies, waits for them, and re-layouts  5 us
    pallas_call x1, Pallas kernels, spectra(): pl.pallas_call(spectrum_kernel, grid=(channels // block,), out_shape=jax....  4.67 us
    convert_element_type x1, other arithmetic, per_device(): return cross(weighted, groups, parts).astype(F32)  4.17 us
    another operation x1, other arithmetic  1.91 us

profile of v3, /device:TPU:0, one launch (start us, length us, event | category | flops | bytes accessed | tf_op | source)
XLA Modules:
  0.0 80.4 jit_solution(2561610068125601135)
XLA Ops:
  0.0 0.8 select_reduce_fusion
  0.8 0.7 convert_rsqrt_fusion
  1.5 1.9 %multiply_convert_fusion.1 = (bf16[64,1024]{1,0:T(8,128)(2,1)S(1)}, bf16[64,1024]{1,0:T(8,128)(2,1)S(1)}) fusion(s32[64]{0:T(128)} %param.8, f32[1024]{0:T(1024)S(1)} %get-tuple-element.7, f32[1024]{0:T(1024)S(1)} %get-tuple-element.8), kind=kLoop, calls=%fused_computation.8 | loop fusion | flops 1179648 | bytes 270592 | tf_op jit(solution)/shard_map/convert
  3.4 0.0 copy-start
  3.4 3.4 %copy-done = bf16[64,64,1024]{2,1,0:T(8,128)(2,1)S(1)} copy-done((bf16[64,64,1024]{2,1,0:T(8,128)(2,1)S(1)}, bf16[64,64,1024]{2,1,0:T(8,128)(2,1)}, u32[]{:S(2)}) %copy-start) | copy-done | bytes 8388632
  6.8 0.0 copy-start.2
  6.8 0.7 copy-done.2
  7.5 4.7 %shard_map.55 = bf16[64,64,128]{2,1,0:T(8,128)(2,1)S(1)} custom-call(f32[64]{0:T(128)S(1)} %get-tuple-element.10.limit_ref, s32[64]{0:T(128)S(1)} %copy-done.2, f32[64]{0:T(128)S(1)} %get-tuple-element.9.root_ref, bf16[128,1024]{1,0:T(8,128)(2,1)S(1)} %pad_maximum_fusion.table_ref, bf16[64,64,1024]{2,1,0:T(8,128)(2,1)S(1)} %copy-done), custom_call_target="tpu_custom_call" | custom-call | tf_op jit(solution)/shard_map/pallas_call | solution.py:62
  12.1 0.0 copy-start.1
  12.1 1.0 %copy-done.1 = bf16[64,64,128]{2,1,0:T(8,128)(2,1)} copy-done((bf16[64,64,128]{2,1,0:T(8,128)(2,1)}, bf16[64,64,128]{2,1,0:T(8,128)(2,1)S(1)}, u32[]{:S(2)}) %copy-start.1) | copy-done | bytes 1048600
  13.1 63.1 %shard_map.56 = bf16[16,2,64,512]{3,2,1,0:T(8,128)(2,1)} custom-call(bf16[8,8,64,128]{3,2,1,0:T(8,128)(2,1)} %bitcast.1), custom_call_target="tpu_custom_call" | custom-call | tf_op jit(solution)/shard_map/pallas_call | solution.py:340
  76.2 4.2 %convert_element_type.25 = f32[16,2,64,512]{3,2,1,0:T(8,128)} convert(bf16[16,2,64,512]{3,2,1,0:T(8,128)(2,1)} %shard_map.56) | non-fusion elementwise | flops 1048576 | bytes 6291456 | tf_op jit(solution)/shard_map/convert_element_type | solution.py:374
  (2 shorter events, 0.1 us)
Async XLA Ops:
  3.4 3.4 %copy-start = (bf16[64,64,1024]{2,1,0:T(8,128)(2,1)S(1)}, bf16[64,64,1024]{2,1,0:T(8,128)(2,1)}, u32[]{:S(2)}) copy-start(bf16[64,64,1024]{2,1,0:T(8,128)(2,1)} %strain_ref.1) | copy-start | bytes 25165828
  6.8 0.7 copy-start.2
  12.1 1.0 %copy-start.1 = (bf16[64,64,128]{2,1,0:T(8,128)(2,1)}, bf16[64,64,128]{2,1,0:T(8,128)(2,1)S(1)}, u32[]{:S(2)}) copy-start(bf16[64,64,128]{2,1,0:T(8,128)(2,1)S(1)} %shard_map.55) | copy-start | bytes 3145732

commit v4 on v3

--- a/solution.py
+++ b/solution.py
@@ -25,13 +25,13 @@
     return jnp.concatenate([cosine, sine], axis=0).astype(BF16)
 
 
-def spectrum_kernel(limit_ref, count_ref, root_ref, table_ref, strain_ref, out_ref):
+def spectrum_kernel(index_ref, scale_ref, count_ref, table_ref, strain_ref, out_ref):
     block, wins, length = strain_ref.shape
     bins = out_ref.shape[0]
     first = pl.program_id(0) * block
     clipped = []
     for c in range(block):
-        limit = jnp.full((wins, 128), limit_ref[first + c], F32).astype(BF16)
+        limit = jnp.full((wins, 128), scale_ref[index_ref[first + c]] * CLIP_FACTOR, F32).astype(BF16)
         limit = jnp.concatenate([limit] * (length // 128), axis=1)
         clipped.append(jnp.minimum(jnp.maximum(strain_ref[c], -limit), limit))
     rows = jnp.concatenate(clipped, axis=0)
@@ -49,12 +49,13 @@
         odd = jnp.where(low, pltpu.roll(re, wins, 1), im)
         for d, both in enumerate((even, odd)):
             channel = first + c + d
-            weight = jnp.where(window < count_ref[channel], root_ref[channel], 0.0)
+            root = 1.0 / jnp.sqrt(jnp.full((1, 2 * wins), count_ref[channel], jnp.int32).astype(F32))
+            weight = jnp.where(window < count_ref[channel], root, 0.0)
             weighted.append(both * weight)
     out_ref[...] = jnp.swapaxes(jnp.stack(weighted), 0, 1).astype(BF16)
 
 
-def spectra(strain, limits, valid_count, roots, table):
+def spectra(strain, mad_index, mad_table, valid_count, table):
     channels, wins, length = strain.shape
     bins = table.shape[0] // 2
     block = 16
@@ -72,7 +73,7 @@
         ],
         out_specs=pl.BlockSpec((bins, block, 2 * wins), lambda i: (0, i, 0)),
         compiler_params=pltpu.CompilerParams(vmem_limit_bytes=32 * 2**20),
-    )(limits, valid_count, roots, table, strain)
+    )(mad_index, mad_table, valid_count, table, strain)
 
 
 def cross_kernel(groups, parts, cuts, w_ref, o_ref, panel, left, left_end, stage, stage_end, own_sem, a_send,
@@ -248,18 +249,35 @@
 
     def step(s, carry):
         lower, upper = z - 1 - s, z + 1 + s
-        for h in range(cuts):
-            @pl.when(lower >= 0)
+        in_low_half = z * 2 < groups
+
+        def take_low(h, wanted):
+            @pl.when(wanted & (lower >= 0))
             def _():
                 for k in range(pieces):
                     along(lower, k, h, up_send, above).wait_recv()
                     pass_up(lower, k, h)
 
-            @pl.when(upper <= last)
+        def take_high(h, wanted):
+            @pl.when(wanted & (upper <= last))
             def _():
                 for k in range(pieces):
                     along(upper, k, h, down_send, below).wait_recv()
                     pass_down(upper, k, h)
+
+        def take_near(h):
+            take_low(h, in_low_half)
+            take_high(h, z * 2 >= groups)
+
+        def take_far(h):
+            take_high(h, in_low_half)
+            take_low(h, z * 2 >= groups)
+
+        take_near(0)
+        for h in range(cuts):
+            if h + 1 < cuts:
+                take_near(h + 1)
+            take_far(h)
 
             @pl.when(is_helper & (s == 0))
             def _():
@@ -362,12 +380,8 @@
 def per_device(strain, mad_index, mad_table, freq_bins, valid_count):
     channels, wins, length = strain.shape
     bins = freq_bins.shape[0]
-    entries = jnp.arange(mad_table.shape[0], dtype=jnp.int32)
-    matches = mad_index[:, None] == entries[None, :]
-    limits = jnp.sum(jnp.where(matches, mad_table[None, :], 0.0), axis=1) * CLIP_FACTOR
-    roots = 1.0 / jnp.sqrt(valid_count.astype(F32))
     table = dft_rows(freq_bins, length)
-    weighted = spectra(strain, limits, valid_count, roots, table)
+    weighted = spectra(strain, mad_index, mad_table, valid_count, table)
     parts, groups = lax.axis_size("freq"), lax.axis_size("chan") // PAIR
     pieces = parts * PAIR
     weighted = weighted.reshape(pieces, bins // pieces, channels, 2 * wins)

time: 80.6 us -> 80.5 us (level)
  other arithmetic: 7.56 us -> 6.15 us
  local copies, waits for them, and re-layouts: 5 us -> 6.31 us
    unnamed x6 -> x10, local copies, waits for them, and re-layouts: 5 us -> 6.31 us
where the time goes in v4:
time: 80.5 us; the launch traced here: 80.3 us
  Pallas kernels  67.8 us (84%)
  local copies, waits for them, and re-layouts  6.31 us (8%)
  other arithmetic  6.15 us (8%)
    pallas_call x1, Pallas kernels, cross(): pl.pallas_call(functools.partial(cross_kernel, groups, parts, cuts), out_...  63.1 us
    unnamed x10, local copies, waits for them, and re-layouts  6.31 us
    pallas_call x1, Pallas kernels, spectra(): pl.pallas_call(spectrum_kernel, grid=(channels // block,), out_shape=jax....  4.67 us
    convert_element_type x1, other arithmetic, per_device(): return cross(weighted, groups, parts).astype(F32)  4.17 us
    another operation x1, other arithmetic  1.91 us

profile of v4, /device:TPU:0, one launch (start us, length us, event | category | flops | bytes accessed | tf_op | source)
XLA Modules:
  0.0 80.3 jit_solution(4193975250630621268)
XLA Ops:
  0.0 1.9 %multiply_convert_fusion.1 = (bf16[64,1024]{1,0:T(8,128)(2,1)S(1)}, bf16[64,1024]{1,0:T(8,128)(2,1)S(1)}) fusion(s32[64]{0:T(128)} %param.8, f32[1024]{0:T(1024)S(1)} %get-tuple-element.7, f32[1024]{0:T(1024)S(1)} %get-tuple-element.8), kind=kLoop, calls=%fused_computation.8 | loop fusion | flops 1179648 | bytes 270592 | tf_op jit(solution)/shard_map/convert
  2.0 0.0 copy-start
  2.0 3.4 %copy-done = bf16[64,64,1024]{2,1,0:T(8,128)(2,1)S(1)} copy-done((bf16[64,64,1024]{2,1,0:T(8,128)(2,1)S(1)}, bf16[64,64,1024]{2,1,0:T(8,128)(2,1)}, u32[]{:S(2)}) %copy-start) | copy-done | bytes 8388632
  5.4 0.0 copy-start.2
  5.4 0.7 copy-done.2
  6.0 0.0 copy-start.3
  6.0 0.7 copy-done.3
  6.7 0.0 copy-start.4
  6.7 0.7 copy-done.4
  7.3 4.7 %shard_map.55 = bf16[64,64,128]{2,1,0:T(8,128)(2,1)S(1)} custom-call(s32[64]{0:T(128)S(1)} %copy-done.2, f32[16]{0:T(128)S(1)} %copy-done.3, s32[64]{0:T(128)S(1)} %copy-done.4, bf16[128,1024]{1,0:T(8,128)(2,1)S(1)} %pad_maximum_fusion.table_ref, bf16[64,64,1024]{2,1,0:T(8,128)(2,1)S(1)} %copy-done), custom_call_target="tpu_custom_call" | custom-call | tf_op jit(solution)/shard_map/pallas_call | solution.py:63
  12.0 0.0 copy-start.1
  12.0 1.0 %copy-done.1 = bf16[64,64,128]{2,1,0:T(8,128)(2,1)} copy-done((bf16[64,64,128]{2,1,0:T(8,128)(2,1)}, bf16[64,64,128]{2,1,0:T(8,128)(2,1)S(1)}, u32[]{:S(2)}) %copy-start.1) | copy-done | bytes 1048600
  13.0 63.1 %shard_map.56 = bf16[16,2,64,512]{3,2,1,0:T(8,128)(2,1)} custom-call(bf16[8,8,64,128]{3,2,1,0:T(8,128)(2,1)} %bitcast.1), custom_call_target="tpu_custom_call" | custom-call | tf_op jit(solution)/shard_map/pallas_call | solution.py:358
  76.1 4.2 %convert_element_type.21 = f32[16,2,64,512]{3,2,1,0:T(8,128)} convert(bf16[16,2,64,512]{3,2,1,0:T(8,128)(2,1)} %shard_map.56) | non-fusion elementwise | flops 1048576 | bytes 6291456 | tf_op jit(solution)/shard_map/convert_element_type | solution.py:388
  (2 shorter events, 0.1 us)
Async XLA Ops:
  2.0 3.4 %copy-start = (bf16[64,64,1024]{2,1,0:T(8,128)(2,1)S(1)}, bf16[64,64,1024]{2,1,0:T(8,128)(2,1)}, u32[]{:S(2)}) copy-start(bf16[64,64,1024]{2,1,0:T(8,128)(2,1)} %strain_ref.1) | copy-start | bytes 25165828
  5.4 0.7 copy-start.2
  6.0 0.7 copy-start.3
  6.7 0.7 copy-start.4
  12.0 1.0 %copy-start.1 = (bf16[64,64,128]{2,1,0:T(8,128)(2,1)}, bf16[64,64,128]{2,1,0:T(8,128)(2,1)S(1)}, u32[]{:S(2)}) copy-start(bf16[64,64,128]{2,1,0:T(8,128)(2,1)S(1)} %shard_map.55) | copy-start | bytes 3145732

commit v5 on v4

--- a/solution.py
+++ b/solution.py
@@ -25,13 +25,13 @@
     return jnp.concatenate([cosine, sine], axis=0).astype(BF16)
 
 
-def spectrum_kernel(index_ref, scale_ref, count_ref, table_ref, strain_ref, out_ref):
+def spectrum_kernel(facts_ref, table_ref, strain_ref, out_ref):
     block, wins, length = strain_ref.shape
     bins = out_ref.shape[0]
     first = pl.program_id(0) * block
     clipped = []
     for c in range(block):
-        limit = jnp.full((wins, 128), scale_ref[index_ref[first + c]] * CLIP_FACTOR, F32).astype(BF16)
+        limit = jnp.full((wins, 128), facts_ref[0, first + c], F32).astype(BF16)
         limit = jnp.concatenate([limit] * (length // 128), axis=1)
         clipped.append(jnp.minimum(jnp.maximum(strain_ref[c], -limit), limit))
     rows = jnp.concatenate(clipped, axis=0)
@@ -41,6 +41,7 @@
     lane = lax.broadcasted_iota(jnp.int32, (bins, 2 * wins), 1)
     low = lane < wins
     window = lax.axis_index("freq") * wins + lax.rem(lane, wins)
+    window = window.astype(F32)
     weighted = []
     for c in range(0, block, 2):
         re = spectrum[:bins, c * wins : (c + 2) * wins]
@@ -49,13 +50,13 @@
         odd = jnp.where(low, pltpu.roll(re, wins, 1), im)
         for d, both in enumerate((even, odd)):
             channel = first + c + d
-            root = 1.0 / jnp.sqrt(jnp.full((1, 2 * wins), count_ref[channel], jnp.int32).astype(F32))
-            weight = jnp.where(window < count_ref[channel], root, 0.0)
+            root = 1.0 / jnp.sqrt(jnp.full((1, 2 * wins), facts_ref[1, channel], F32))
+            weight = jnp.where(window < facts_ref[1, channel], root, 0.0)
             weighted.append(both * weight)
     out_ref[...] = jnp.swapaxes(jnp.stack(weighted), 0, 1).astype(BF16)
 
 
-def spectra(strain, mad_index, mad_table, valid_count, table):
+def spectra(strain, facts, table):
     channels, wins, length = strain.shape
     bins = table.shape[0] // 2
     block = 16
@@ -66,14 +67,12 @@
         out_shape=jax.ShapeDtypeStruct((bins, channels, 2 * wins), BF16),
         in_specs=[
             smem,
-            smem,
-            smem,
             pl.BlockSpec((2 * bins, length), lambda i: (0, 0)),
             pl.BlockSpec((block, wins, length), lambda i: (i, 0, 0)),
         ],
         out_specs=pl.BlockSpec((bins, block, 2 * wins), lambda i: (0, i, 0)),
         compiler_params=pltpu.CompilerParams(vmem_limit_bytes=32 * 2**20),
-    )(mad_index, mad_table, valid_count, table, strain)
+    )(facts, table, strain)
 
 
 def cross_kernel(groups, parts, cuts, w_ref, o_ref, panel, left, left_end, stage, stage_end, own_sem, a_send,
@@ -358,7 +357,7 @@
     return pl.pallas_call(
         functools.partial(cross_kernel, groups, parts, cuts),
         out_shape=jax.ShapeDtypeStruct((PAIR * bins, 2, rows, groups * PAIR * rows), BF16),
-        in_specs=[pl.BlockSpec(memory_space=pl.ANY)],
+        in_specs=[pl.BlockSpec(memory_space=pltpu.VMEM)],
         out_specs=pl.BlockSpec(memory_space=pltpu.VMEM),
         scratch_shapes=[
             pltpu.VMEM((groups, pieces, bins, rows, lanes), BF16),
@@ -372,7 +371,7 @@
             dma((groups, PAIR, cuts)), dma((groups, PAIR, cuts)),
         ],
         compiler_params=pltpu.CompilerParams(
-            collective_id=0, has_side_effects=True, vmem_limit_bytes=56 * 2**20
+            collective_id=0, has_side_effects=True, vmem_limit_bytes=(3 * groups + 12) * 2**20
         ),
     )(weighted)
 
@@ -381,7 +380,11 @@
     channels, wins, length = strain.shape
     bins = freq_bins.shape[0]
     table = dft_rows(freq_bins, length)
-    weighted = spectra(strain, mad_index, mad_table, valid_count, table)
+    entries = jnp.arange(mad_table.shape[0], dtype=jnp.int32)
+    matches = mad_index[:, None] == entries[None, :]
+    limits = jnp.sum(jnp.where(matches, mad_table[None, :], 0.0), axis=1) * CLIP_FACTOR
+    facts = jnp.stack([limits, valid_count.astype(F32)])
+    weighted = spectra(strain, facts, table)
     parts, groups = lax.axis_size("freq"), lax.axis_size("chan") // PAIR
     pieces = parts * PAIR
     weighted = weighted.reshape(pieces, bins // pieces, channels, 2 * wins)

time: 80.5 us -> 76.1 us (0.945)
  local copies, waits for them, and re-layouts: 6.31 us -> 3.38 us
  Pallas kernels: 67.8 us -> 66.5 us
    unnamed x10 -> x2, local copies, waits for them, and re-layouts: 6.31 us -> 3.38 us
    convert_element_type x1, other arithmetic: 4.17 us -> 2.58 us  [per_device(): return cross(weighted, groups, parts).astype(F32)]
    pallas_call x1, Pallas kernels: 63.1 us -> 61.9 us  [cross(): pl.pallas_call(functools.partial(cross_kernel, groups, parts, cuts), out_...]
    another operation x1 -> x3, other arithmetic: 1.91 us -> 2.58 us
where the time goes in v5:
time: 76.1 us; the launch traced here: 76 us
  Pallas kernels  66.5 us (87%)
  other arithmetic  5.99 us (8%)
  local copies, waits for them, and re-layouts  3.38 us (4%)
    pallas_call x1, Pallas kernels, cross(): pl.pallas_call(functools.partial(cross_kernel, groups, parts, cuts), out_...  61.9 us
    pallas_call x1, Pallas kernels, spectra(): pl.pallas_call(spectrum_kernel, grid=(channels // block,), out_shape=jax....  4.67 us
    unnamed x2, local copies, waits for them, and re-layouts  3.38 us
    convert_element_type x1, other arithmetic, per_device(): return cross(weighted, groups, parts).astype(F32)  2.58 us
    another operation x1, other arithmetic  1.91 us

profile of v5, /device:TPU:0, one launch (start us, length us, event | category | flops | bytes accessed | tf_op | source)
XLA Modules:
  0.0 76.0 jit_solution(242437830827894003)
XLA Ops:
  0.0 0.8 select_reduce_fusion
  0.8 0.7 convert_bitcast_fusion
  1.5 1.9 %multiply_convert_fusion.1 = (bf16[64,1024]{1,0:T(8,128)(2,1)S(1)}, bf16[64,1024]{1,0:T(8,128)(2,1)S(1)}) fusion(s32[64]{0:T(128)} %param.8, f32[1024]{0:T(1024)S(1)} %get-tuple-element.7, f32[1024]{0:T(1024)S(1)} %get-tuple-element.8), kind=kLoop, calls=%fused_computation.8 | loop fusion | flops 1179648 | bytes 270592 | tf_op jit(solution)/shard_map/convert
  3.4 0.0 copy-start
  3.4 3.4 %copy-done = bf16[64,64,1024]{2,1,0:T(8,128)(2,1)S(1)} copy-done((bf16[64,64,1024]{2,1,0:T(8,128)(2,1)S(1)}, bf16[64,64,1024]{2,1,0:T(8,128)(2,1)}, u32[]{:S(2)}) %copy-start) | copy-done | bytes 8388632
  6.8 4.7 %shard_map.55 = bf16[64,64,128]{2,1,0:T(8,128)(2,1)S(1)} custom-call(f32[2,64]{1,0:T(2,128)S(1)} %pad_maximum_fusion.1.facts_ref, bf16[128,1024]{1,0:T(8,128)(2,1)S(1)} %pad_maximum_fusion.table_ref, bf16[64,64,1024]{2,1,0:T(8,128)(2,1)S(1)} %copy-done), custom_call_target="tpu_custom_call" | custom-call | tf_op jit(solution)/shard_map/pallas_call | solution.py:64
  11.5 61.9 %shard_map.56 = bf16[16,2,64,512]{3,2,1,0:T(8,128)(2,1)S(1)} custom-call(bf16[8,8,64,128]{3,2,1,0:T(8,128)(2,1)S(1)} %bitcast.5), custom_call_target="tpu_custom_call" | custom-call | tf_op jit(solution)/shard_map/pallas_call | solution.py:357
  73.4 2.6 %convert_element_type.25 = f32[16,2,64,512]{3,2,1,0:T(8,128)} convert(bf16[16,2,64,512]{3,2,1,0:T(8,128)(2,1)S(1)} %shard_map.56) | non-fusion elementwise | flops 1048576 | bytes 6291456 | tf_op jit(solution)/shard_map/convert_element_type | solution.py:391
  (4 shorter events, 0.1 us)
Async XLA Ops:
  3.4 3.4 %copy-start = (bf16[64,64,1024]{2,1,0:T(8,128)(2,1)S(1)}, bf16[64,64,1024]{2,1,0:T(8,128)(2,1)}, u32[]{:S(2)}) copy-start(bf16[64,64,1024]{2,1,0:T(8,128)(2,1)} %strain_ref.1) | copy-start | bytes 25165828
